TPU v7x, 512 devices: a whole 4x4x16 slice. The times are simulated.
512 devices in a mesh: gen: 64 (over z, y), net: 8 (over x, core).
Axes of the slice: x: 4, y: 4, z: 16, core: 2. Of those that a mesh axis runs over, the one named last changes fastest.
Arguments:
- state: float32 [6, 256, 16384], P(None, 'net', 'gen'), as said below
- params: float32 [13, 16384], P(None, 'gen'), as said below
- gen_count: int32 [64], P('gen'), may hold values from 1 to 256, 12288 in all
- gen_block: int32 [16384, 1], P('gen'), may hold values from 0 to 63; in each aligned block of 256 rows (0 to 255, 256 to 511, ...) at most 6 rows name the same one
- gen_local: int32 [16384], P('gen'), may hold values from 0 to 191
- impedance: bfloat16 [2, 12288, 24576], P(None, 'net', 'gen')
- fault_bus: int32 [256], P('net'), may hold values from 0 to 12287
- cleared: int32 [256], P('net'), may hold values 0 or 1
- fault_volt: float32 [2, 256], P(None, 'net'), may hold values from -0.3 to 0.3
Outputs:
- slope: float32 [6, 256, 16384], P(None, 'net', 'gen')
Inputs may be any that keep to these rules, and one draw needn't show every extreme that they name: `gen_block`: among the 256 slots of one gen index, at most 6 name one bus block. Entries lie in the ranges of the state rows: angle within pi, speed deviation within 0.6, emfs and field voltage positive except the d subtransient emf. `params`: reactances satisfy Xd > Xdt > Xs and Xq > Xs; all parameters are positive.
All inputs are finite; a program needn't handle non-finite values. No bound on the sum of `gen_count` or of `cleared` on one device may be relied on, other than what follows from the above.
Results may differ from a plain program's by a relative error of at most 0.00065.
The roundings to bfloat16 on the way count: a program that leaves them out, or rounds other values in their place, can miss the bound.
Values may be sent and summed in bfloat16 or wider, within the bound.
A program may use at most 64 MiB of HBM per device.

v0:
```python
import jax
import jax.numpy as jnp
from jax import lax
from jax.sharding import PartitionSpec as P


def machine_emf(state):
    delta, eq_s, ed_s = (state[0], state[3], state[4])
    sin_d = jnp.sin(delta)
    cos_d = jnp.cos(delta)
    emf_re = ed_s * sin_d + eq_s * cos_d
    emf_im = eq_s * sin_d - ed_s * cos_d
    return (sin_d, cos_d, emf_re, emf_im)


def machine_slope(state, params, active, volt_re, volt_im):
    sin_d, cos_d, emf_re, emf_im = machine_emf(state)
    omega, eq_t, eq_s, ed_s, efd = (state[1], state[2], state[3], state[4], state[5])
    sub_x = params[7]
    gen_re = (emf_im - volt_im) / sub_x
    gen_im = (volt_re - emf_re) / sub_x
    cur_d = gen_re * sin_d - gen_im * cos_d
    cur_q = gen_re * cos_d + gen_im * sin_d
    power = ed_s * cur_d + eq_s * cur_q
    term = jnp.sqrt(volt_re * volt_re + volt_im * volt_im + 0.01)
    second = (params[12] - power - params[1] * omega) / (2.0 * params[0])
    third = (efd - eq_t - (params[5] - params[6]) * cur_d) / params[2]
    fourth = (eq_t - eq_s - (params[6] - sub_x) * cur_d) / params[3]
    fifth = ((params[8] - sub_x) * cur_q - ed_s) / params[4]
    sixth = (params[9] * (params[11] - term) - efd) / params[10]
    return jnp.stack([omega, second, third, fourth, fifth, sixth]) * active


def body(state, params, gen_count, gen_block, gen_local, impedance, fault_bus, cleared, fault_volt):
    highest = lax.Precision.HIGHEST
    n_cols = lax.axis_size("gen")
    scen_dev = state.shape[1]
    slot_count = state.shape[2]
    bus_dev = impedance.shape[2] // 2
    send_cap = max(2, 3 * slot_count // (2 * n_cols))
    boxes = n_cols * send_cap
    slot_ids = jnp.arange(slot_count, dtype=jnp.int32)
    active = (slot_ids < gen_count[0]).astype(jnp.float32)
    sin_d, cos_d, emf_re, emf_im = machine_emf(state)
    sub_x = params[7]
    norton_re = emf_im / sub_x * active
    norton_im = -emf_re / sub_x * active
    currents = jnp.concatenate([norton_re, norton_im], axis=0).T
    target = gen_block[:, 0]
    earlier = (target[:, None] == target[None, :]) & (slot_ids[None, :] < slot_ids[:, None])
    rank = jnp.sum(earlier.astype(jnp.int32), axis=1)
    position = target * send_cap + rank
    box_hit = jnp.arange(boxes, dtype=jnp.int32)[:, None] == position[None, :]
    send_hot = box_hit.astype(jnp.float32)
    box_ids = jnp.sum(jnp.where(box_hit, gen_local[None, :] + 1, 0), axis=1) - 1
    box_cur = jnp.dot(send_hot, currents, precision=highest, preferred_element_type=jnp.float32)
    recv_cur, recv_ids = (
        lax.all_to_all(
            box_cur.reshape(n_cols, send_cap, 2 * scen_dev),
            "gen",
            split_axis=0,
            concat_axis=0,
            tiled=True,
        ),
        lax.all_to_all(
            box_ids.reshape(n_cols, send_cap), "gen", split_axis=0, concat_axis=0, tiled=True
        ),
    )
    recv_cur = recv_cur.reshape(boxes, 2 * scen_dev)
    recv_ids = recv_ids.reshape(boxes)
    bus_hot = (recv_ids[:, None] == jnp.arange(bus_dev, dtype=jnp.int32)[None, :]).astype(
        jnp.float32
    )
    summed_bus = lax.dot_general(
        recv_cur,
        bus_hot,
        (((0,), (0,)), ((), ())),
        precision=highest,
        preferred_element_type=jnp.float32,
    )
    column = lax.axis_index("gen")
    fault_on = (fault_bus // bus_dev == column) & (cleared == 0)
    fault_hot = (
        fault_on[:, None]
        & ((fault_bus % bus_dev)[:, None] == jnp.arange(bus_dev, dtype=jnp.int32)[None, :])
    ).astype(jnp.float32)
    injected = (
        summed_bus.reshape(2, scen_dev, bus_dev) - 10.0 * fault_volt[:, :, None] * fault_hot[None]
    )
    injected = injected.astype(jnp.bfloat16)
    regrouped = lax.all_to_all(injected, "net", split_axis=2, concat_axis=1, tiled=True)
    total_scen = regrouped.shape[1]
    flat_partial = jnp.einsum(
        "psr,prk->sk",
        lax.all_gather(regrouped, "gen", axis=2, tiled=True),
        impedance,
        preferred_element_type=jnp.float32,
    )
    partial_volts = flat_partial.reshape(total_scen, 2, bus_dev)
    whole_volts = lax.psum(partial_volts, "net")
    volts = lax.dynamic_slice_in_dim(whole_volts, lax.axis_index("net") * scen_dev, scen_dev, 0)
    every_bus = lax.all_gather(volts, "gen", axis=2, tiled=True)
    bus_index = target * bus_dev + gen_local
    at_gen = jnp.take(every_bus, bus_index, axis=2).transpose(1, 0, 2)
    return machine_slope(state, params, active, at_gen[0], at_gen[1])


def solution(mesh):
    in_specs = (
        P(None, "net", "gen"),
        P(None, "gen"),
        P("gen"),
        P("gen", None),
        P("gen"),
        P(None, "net", "gen"),
        P("net"),
        P("net"),
        P(None, "net"),
    )
    out_specs = P(None, "net", "gen")
    return jax.shard_map(body, mesh=mesh, in_specs=in_specs, out_specs=out_specs, check_vma=False)
```

profile of v0, /device:TPU:1, one launch (start us, length us, event | category | flops | bytes accessed | tf_op | source)
XLA Modules:
  0.0 465.3 jit_solution(15380647665312758419)
XLA Ops:
  6.5 1.0 convert_reduce_fusion
  7.6 0.7 multiply_add_fusion.2
  8.3 0.1 select_reduce_fusion
  8.4 0.7 sub.113
  9.2 19.3 %all-to-all-start.1 = ((s32[64,1,6]{2,1,0:T(1,128)}), s32[64,1,6]{2,1,0:T(1,128)S(1)}, u32[]{:S(2)}, u32[]{:S(2)}) async-start(s32[64,1,6]{2,1,0:T(1,128)} %bitcast.8), calls=%async_computation.1 | async-start | bytes 65536 | tf_op jit(solution)/shard_map/all_to_all | solution.py:65
  29.1 0.7 broadcast_multiply_fusion.1
  29.8 1.0 fusion.15
  30.8 0.9 fusion.11
  31.8 0.3 fusion.1
  32.1 0.7 compare_and_fusion
  32.8 0.8 reshape.240
  33.6 8.5 %all-to-all-done.1 = s32[64,1,6]{2,1,0:T(1,128)S(1)} async-done(((s32[64,1,6]{2,1,0:T(1,128)}), s32[64,1,6]{2,1,0:T(1,128)S(1)}, u32[]{:S(2)}, u32[]{:S(2)}) %all-to-all-start.1) | async-done | bytes 1568 | tf_op jit(solution)/shard_map/all_to_all | solution.py:65
  42.1 6.0 %all-to-all-start = ((f32[64,1,384]{2,1,0:T(1,128)}), f32[64,1,384]{2,1,0:T(1,128)S(1)}, u32[]{:S(2)}, u32[]{:S(2)}) async-start(f32[64,1,384]{2,1,0:T(1,128)} %reshape.240), calls=%async_computation | async-start | bytes 196608 | tf_op jit(solution)/shard_map/all_to_all | solution.py:58
  48.1 0.0 all-gather.3.cloned.1.call-start
  48.2 0.7 and_select_fusion
  48.8 0.1 fusion.13
  48.9 0.5 broadcast.157
  49.4 0.6 reduce.3
  50.1 0.1 eq.76
  50.2 12.4 %all-to-all-done = f32[64,1,384]{2,1,0:T(1,128)S(1)} async-done(((f32[64,1,384]{2,1,0:T(1,128)}), f32[64,1,384]{2,1,0:T(1,128)S(1)}, u32[]{:S(2)}, u32[]{:S(2)}) %all-to-all-start) | async-done | bytes 98336 | tf_op jit(solution)/shard_map/all_to_all | solution.py:58
  62.6 0.5 broadcast.158
  63.2 0.9 reduce.4
  64.0 0.1 reshape.241
  64.2 0.1 copy.139
  64.3 0.3 fusion
  64.6 0.1 copy.141
  64.8 0.1 reshape.242
  64.9 11.7 %all_to_all.29 = bf16[8,2,768]{2,1,0:T(2,128)(2,1)S(1)} all-to-all(bf16[8,2,768]{2,1,0:T(2,128)(2,1)S(1)} %reshape.242), channel_id=1, replica_groups=mesh['gen'=64,'net'=8] {'net'}, dimensions={0} | all-to-all | bytes 49152 | tf_op jit(solution)/shard_map/all_to_all | solution.py:91
  76.6 0.1 reshape.243
  76.7 0.7 all_to_all.25
  77.4 0.0 all-gather.3.cloned.1.call-update
  77.5 0.0 copy-start.2
  77.5 0.0 copy-start.3
  77.5 0.0 copy-start.1
  77.5 0.0 all-reduce.2.cloned.1.call-start
  77.6 118.7 %all-gather.3.cloned.1.call-done = bf16[2,256,1536]{1,2,0:T(8,128)(2,1)} async-done(((bf16[2,256,24]{1,2,0:T(8,128)(2,1)}), bf16[2,256,1536]{1,2,0:T(8,128)(2,1)}) %all-gather.3.cloned.1.call-update) | async-done | bytes 1572880 | tf_op jit(solution)/shard_map/all_gather | solution.py:95
  196.2 3.2 fusion.16
  199.4 0.0 all-reduce.2.cloned.1.call-update
  199.4 0.0 all-gather.5.cloned.1.call-start
  199.5 79.5 %all-reduce.2.cloned.1.call-done = f32[256,2,192]{0,2,1:T(8,128)} async-done(((f32[256,2,192]{0,2,1:T(8,128)}), f32[256,2,192]{0,2,1:T(8,128)}) %all-reduce.2.cloned.1.call-update) | async-done | bytes 393232 | tf_op jit(solution)/shard_map/psum | solution.py:100
  279.0 1.0 constant_dynamic-slice_fusion
  280.1 0.8 copy.145
  280.9 0.0 all-gather.5.cloned.1.call-update
  281.0 171.1 %all-gather.5.cloned.1.call-done = f32[32,2,12288]{0,1,2:T(2,128)} async-done(((f32[32,2,192]{0,1,2:T(2,128)}), f32[32,2,12288]{0,1,2:T(2,128)}) %all-gather.5.cloned.1.call-update) | async-done | bytes 3145744 | tf_op jit(solution)/shard_map/all_gather | solution.py:102
  452.1 5.6 %gather_fusion = f32[256,32,2]{1,2,0:T(2,128)S(1)} fusion(f32[32,2,12288]{0,1,2:T(2,128)} %all-gather.5.cloned.1.call-done, s32[1024]{0:T(1024)S(1)} %pad_clamp_fusion), kind=kCustom, calls=%fused_computation | custom fusion | bytes 132096 | tf_op jit(solution)/shard_map/jit(_take)/gather | solution.py:104
  457.7 0.1 copy.146
  457.8 0.2 divide_dynamic-update-slice_fusion.4
  458.1 0.7 broadcast_multiply_fusion
  (18 shorter events, 0.2 us)
Async XLA Ops:
  6.5 189.7 %copy-start = (bf16[2,1536,384]{2,1,0:T(8,128)(2,1)S(1)}, bf16[2,1536,384]{2,1,0:T(8,128)(2,1)}, u32[]{:S(2)}) copy-start(bf16[2,1536,384]{2,1,0:T(8,128)(2,1)} %param.14) | copy-start | bytes 7077892
  9.2 32.9 %all-to-all-start.1 = ((s32[64,1,6]{2,1,0:T(1,128)}), s32[64,1,6]{2,1,0:T(1,128)S(1)}, u32[]{:S(2)}, u32[]{:S(2)}) async-start(s32[64,1,6]{2,1,0:T(1,128)} %bitcast.8), calls=%async_computation.1 | async-start | bytes 65536 | tf_op jit(solution)/shard_map/all_to_all | solution.py:65
  42.1 20.6 %all-to-all-start = ((f32[64,1,384]{2,1,0:T(1,128)}), f32[64,1,384]{2,1,0:T(1,128)S(1)}, u32[]{:S(2)}, u32[]{:S(2)}) async-start(f32[64,1,384]{2,1,0:T(1,128)} %reshape.240), calls=%async_computation | async-start | bytes 196608 | tf_op jit(solution)/shard_map/all_to_all | solution.py:58
  48.1 148.1 %all-gather.3.cloned.1.call-start = ((), (), s32[]{:S(2)}) async-start(), calls=%async_computation.3 | async-start | bytes 1597440 | tf_op jit(solution)/shard_map/all_gather | solution.py:95
  77.5 203.4 %copy-start.2 = (s32[256,1]{0,1:T(1,128)S(1)}, s32[256,1]{0,1:T(1,128)}, u32[]{:S(2)}) copy-start(s32[256,1]{0,1:T(1,128)} %param.12) | copy-start | bytes 3076
  77.5 203.4 %copy-start.3 = (s32[256]{0:T(256)S(1)}, s32[256]{0:T(256)}, u32[]{:S(2)}) copy-start(s32[256]{0:T(256)} %param.13) | copy-start | bytes 3076
  77.5 203.5 %copy-start.1 = (f32[6,32,256]{2,1,0:T(8,128)S(1)}, f32[6,32,256]{2,1,0:T(8,128)}, u32[]{:S(2)}) copy-start(f32[6,32,256]{2,1,0:T(8,128)} %param.9) | copy-start | bytes 589828
  77.5 201.5 %all-reduce.2.cloned.1.call-start = ((), (), s32[]{:S(2)}) async-start(), calls=%async_computation.4 | async-start | bytes 786432 | tf_op jit(solution)/shard_map/psum | solution.py:100
  199.4 252.7 %all-gather.5.cloned.1.call-start = ((), (), s32[]{:S(2)}) async-start(), calls=%async_computation.5 | async-start | bytes 12779520 | tf_op jit(solution)/shard_map/all_gather | solution.py:102
Sparse Core Ops, SparseCore 0:
  77.6 118.5 all-gather.2
  199.6 79.4 all-reduce.1
  282.4 169.6 all-gather.4
where the time goes:
time: 467 us; the launch traced here: 465 us
  waiting for transfers between devices  390 us (84%)
  starting transfers between devices  25.5 us (5%)
  between operations  14 us (3%)
  blocking collectives  11.7 us (3%)
  local copies, waits for them, and re-layouts  11.6 us (2%)
  other arithmetic  8.42 us (2%)
    all_gather x1, waiting for transfers between devices, body(): every_bus = lax.all_gather(volts, 'gen', axis=2, tiled=True)  171 us
    all_gather x1, waiting for transfers between devices, body(): lax.all_gather(regrouped, 'gen', axis=2, tiled=True)  119 us
    psum x1, waiting for transfers between devices, body(): whole_volts = lax.psum(partial_volts, 'net')  79.5 us
    all_to_all x1, starting transfers between devices, body(): lax.all_to_all(box_ids.reshape(n_cols, send_cap), 'gen', split_axis=0, co...  19.3 us
    all_to_all x1, waiting for transfers between devices, body(): lax.all_to_all(box_cur.reshape(n_cols, send_cap, 2 * scen_dev), 'gen', sp...  12.4 us
    all_to_all x1, blocking collectives, body(): lax.all_to_all(injected, 'net', split_axis=2, concat_axis=1, tiled=True)  11.7 us
  transfers between devices with their start and end apart: 5, of which 5 were waited for; matrix products, arithmetic and copies ran while one was open for 1% of the time, Pallas kernels for 0%

commit v1 on v0

v1 whole, which is shorter than its diff:
```python
import functools

import jax
import jax.numpy as jnp
from jax import lax
from jax.experimental import pallas as pl
from jax.experimental.pallas import tpu as pltpu
from jax.sharding import PartitionSpec as P

F32 = jnp.float32
BF16 = jnp.bfloat16
NZ, NY, NX, NCORE = 16, 4, 4, 2
NGEN, NNET = NZ * NY, NX * NCORE
SCN = 32
SLOTS = 256
BUS = 192
SUB = BUS // NNET
CAP = 6
HALF = NZ // 2
NT = (((1,), (1,)), ((), ()))


def remote(src, dst, send_sem, recv_sem, gen, net):
    return pltpu.make_async_remote_copy(
        src_ref=src,
        dst_ref=dst,
        send_sem=send_sem,
        recv_sem=recv_sem,
        device_id=(gen, net),
        device_id_type=pl.DeviceIdType.MESH,
    )


def three(v):
    hi = v.astype(BF16)
    rest = v - hi.astype(F32)
    mid = rest.astype(BF16)
    lo = (rest - mid.astype(F32)).astype(BF16)
    return hi, mid, lo


def lane_iota(shape):
    return lax.broadcasted_iota(jnp.int32, shape, len(shape) - 1)


def row_iota(shape):
    return lax.broadcasted_iota(jnp.int32, shape, 0)


def pack(hot, vals):
    hi, mid, lo = three(vals)
    rhs = jnp.concatenate([hi, mid, lo, lo], axis=0)
    out = lax.dot_general(hot, rhs, NT, preferred_element_type=F32)
    left, right = out[:, :128], out[:, 128:]
    both = left + pltpu.roll(left, 64, 1) + right
    low = lane_iota((NGEN, 128)) < 64
    rows = []
    for j in range(CAP // 2):
        even = both[2 * j * NGEN : (2 * j + 1) * NGEN]
        odd = both[(2 * j + 1) * NGEN : (2 * j + 2) * NGEN]
        rows.append(jnp.where(low, even, odd))
    return rows


def unpack(hot, rows):
    every = jnp.concatenate(rows, axis=0)
    turned = pltpu.roll(every, 64, 1)
    low = lane_iota(every.shape) < 64
    vals = jnp.concatenate([jnp.where(low, every, turned), jnp.where(low, turned, every)], axis=0)
    hi, mid, lo = three(vals)
    first = jnp.where(lane_iota(vals.shape) < 64, hi.astype(F32), mid.astype(F32)).astype(BF16)
    rhs = jnp.concatenate([first, lo], axis=1)
    out = jnp.dot(hot, rhs, preferred_element_type=F32)
    left, right = out[:, :128], out[:, 128:]
    return left + pltpu.roll(left, 64, 1) + right


def kernel(
    state,
    params,
    count,
    block,
    local,
    z_hbm,
    fbus,
    cleared,
    fvolt,
    out,
    zbuf,
    zt,
    gath,
    sbox,
    rbox,
    smsg,
    rmsg,
    vbuf,
    cbuf,
    wbuf,
    xbuf,
    sback,
    rback,
    keep,
    z_sem,
    box_s,
    box_r,
    msg_s,
    msg_r,
    yi_s,
    yi_r,
    zz_s,
    zz_r,
    zy_s,
    zy_r,
    ys_s,
    ys_r,
    yr_s,
    yr_r,
    core_s,
    core_r,
    x_s,
    x_r,
    back_s,
    back_r,
):
    g = lax.axis_index("gen")
    n = lax.axis_index("net")
    z, y = g // NY, g % NY
    x, c = n // NCORE, n % NCORE
    barrier = pltpu.get_barrier_semaphore()

    def greet_gen(i, carry):
        pl.semaphore_signal(
            barrier, inc=1, device_id=((g + i) % NGEN, n), device_id_type=pl.DeviceIdType.MESH
        )
        return carry

    def greet_net(i, carry):
        pl.semaphore_signal(
            barrier, inc=1, device_id=(g, (n + i) % NNET), device_id_type=pl.DeviceIdType.MESH
        )
        return carry

    lax.fori_loop(1, NGEN, greet_gen, 0)
    lax.fori_loop(1, NNET, greet_net, 0)
    z_copy = pltpu.make_async_copy(z_hbm, zbuf, z_sem)
    z_copy.start()

    tgt_s = block[...]
    ii, jj = row_iota((SLOTS, SLOTS)), lane_iota((SLOTS, SLOTS))
    tgt_b = jnp.broadcast_to(tgt_s, (SLOTS, SLOTS)).astype(F32)
    tgt_l = jnp.sum(jnp.where(ii == jj, tgt_b, 0.0), axis=0, keepdims=True)
    same = tgt_b == tgt_l
    rank_l = jnp.sum(jnp.where(same & (ii < jj), 1.0, 0.0), axis=0, keepdims=True)
    rank_s = jnp.sum(jnp.where(same & (jj < ii), 1.0, 0.0), axis=1, keepdims=True).astype(jnp.int32)
    code_l = rank_l * NGEN + tgt_l
    code_s = (rank_s % 2) * (3 * NGEN) + (rank_s // 2) * NGEN + tgt_s
    send_hot = jnp.where(
        row_iota((CAP * NGEN, SLOTS)).astype(F32) == code_l, 1.0, 0.0
    ).astype(BF16)

    active = (lane_iota((1, SLOTS)) < count[0]).astype(F32)
    delta, eq_s, ed_s = state[0], state[3], state[4]
    sin_d = jnp.sin(delta)
    cos_d = jnp.cos(delta)
    emf_re = ed_s * sin_d + eq_s * cos_d
    emf_im = eq_s * sin_d - ed_s * cos_d
    keep[0] = sin_d
    keep[1] = cos_d
    keep[2] = emf_re
    keep[3] = emf_im
    sub_x = params[7:8, :]
    cur = jnp.concatenate([emf_im / sub_x * active, -emf_re / sub_x * active], axis=0)
    for j, row in enumerate(pack(send_hot, cur)):
        sbox[:, j, :] = row
    ids = lax.dot_general(
        send_hot,
        jnp.broadcast_to((local[...] + 1).astype(F32), (128, SLOTS)).astype(BF16),
        NT,
        preferred_element_type=F32,
    )
    lane = lane_iota((NGEN, 128))
    id_row = jnp.zeros((NGEN, 128), F32)
    for r in range(CAP):
        id_row = jnp.where(lane == r, ids[r * NGEN : (r + 1) * NGEN], id_row)
    sbox[:, 3, :] = id_row

    pl.semaphore_wait(barrier, NGEN - 1 + NNET - 1)

    def send_box(i, carry):
        peer = (g + i) % NGEN
        remote(sbox.at[peer], rbox.at[g], box_s, box_r, peer, n).start()
        return carry

    lax.fori_loop(1, NGEN, send_box, 0)
    rbox[g] = sbox[g]
    z_copy.wait()

    def turn(j):
        parts = [zbuf[p, j].astype(F32) for p in range(2)]
        rows = []
        for k in range(8):
            a = k * SUB
            rows += [
                parts[0][a : a + 16],
                parts[1][a : a + 16],
                parts[0][a + 16 : a + 24],
                parts[1][a + 16 : a + 24],
            ]
        zt[j] = jnp.concatenate(rows, axis=0).T.astype(BF16)

    all_boxes = remote(
        sbox.at[pl.ds(0, NGEN - 1)], rbox.at[pl.ds(0, NGEN - 1)], box_s, box_r, g, n
    )
    all_boxes.wait_recv()

    ids_in = rbox[:, 3, :]
    ids_t = ids_in.T
    id_lane = jnp.concatenate([ids_t[r : r + 1] for r in (0, 2, 4, 1, 3, 5)], axis=1)
    row = row_iota((256, 1))
    part, i16 = (row % 128) // 16, row % 16
    bus = part * SUB + jnp.where(row < 128, i16, 16 + i16 % 8)
    bus_hot = jnp.where((bus + 1).astype(F32) == id_lane, 1.0, 0.0).astype(BF16)
    summed = unpack(bus_hot, [rbox[:, j, :] for j in range(3)])
    fb, cl = fbus[...], cleared[...]
    fb4 = jnp.concatenate([fb] * 4, axis=1)
    on4 = 1.0 - jnp.concatenate([cl] * 4, axis=1).astype(F32)
    fv4 = jnp.concatenate([fvolt[0:1], fvolt[1:2]] * 2, axis=1)
    hit = jnp.where(bus + g * BUS == fb4, 1.0, 0.0) * on4
    inject = summed - 10.0 * fv4 * hit
    first, second = inject[:128], inject[128:]
    i16 = row_iota((128, 128)) % 16
    second = jnp.where(i16 < 8, second, pltpu.roll(second, 96, 1))
    message = jnp.where(lane_iota((128, 128)) < 64, first, second).astype(BF16)
    smsg[...] = message.reshape(NNET, 16, 128)

    def send_msg(i, carry):
        peer = (n + i) % NNET
        remote(smsg.at[peer], rmsg.at[n], msg_s, msg_r, g, peer).start()
        return carry

    lax.fori_loop(1, NNET, send_msg, 0)
    rmsg[n] = smsg[n]
    all_msgs = remote(
        smsg.at[pl.ds(0, NNET - 1)], rmsg.at[pl.ds(0, NNET - 1)], msg_s, msg_r, g, n
    )
    all_msgs.wait_recv()
    tiles = [rmsg[k].astype(F32) for k in range(NNET)]
    for j in range(3):
        chunk = jnp.concatenate([t[:, SCN * j : SCN * (j + 1)] for t in tiles], axis=1)
        gath[z, y, j] = chunk.astype(BF16)

    yp, ym = (y + 1) % NY, (y + NY - 1) % NY
    zp, zm = (z + 1) % NZ, (z + NZ - 1) % NZ
    right, left = z * NY + yp, z * NY + ym
    up, down = zp * NY + y, zm * NY + y

    def own(slot):
        return gath.at[slot, y, pl.ds(1, 2)]

    def own_copy(slot, way, t):
        return remote(own(slot), own(slot), zz_s.at[way, t], zz_r.at[way, t], up if way == 0 else down, n)

    def bundle_copy(slot, piece, way, t):
        ref = gath.at[slot, pl.ds(2 * piece, 2), 0]
        return remote(
            ref, ref, zy_s.at[way, piece, t], zy_r.at[way, piece, t], up if way == 0 else down, n
        )

    def side_copy(slot, way, k, arriving=False):
        col = (ym if way == 0 else yp) if arriving else y
        ref = gath.at[slot, col, pl.ds(1, 2)]
        return remote(ref, ref, ys_s.at[way, k], ys_r.at[way, k], right if way == 0 else left, n)

    def relay_copy(slot, way, k, arriving=False):
        if arriving:
            col = (y + 2) % NY
        else:
            col = ym if way == 0 else yp
        ref = gath.at[slot, col, 1 + way]
        return remote(ref, ref, yr_s.at[way, k], yr_r.at[way, k], right if way == 0 else left, n)

    for d in range(1, NY):
        ref = gath.at[z, y, 0]
        remote(ref, ref, yi_s, yi_r, z * NY + (y + d) % NY, n).start()
    for way in range(2):
        own_copy(z, way, 0).start()
    for way in range(2):
        side_copy(z, way, 0).start()
    ref = gath.at[z, pl.ds(0, NY - 1), 0]
    y_first = remote(ref, ref, yi_s, yi_r, g, n)
    y_first.wait_recv()
    for piece in range(2):
        for way in range(2):
            bundle_copy(z, piece, way, 0).start()

    def slot_at(k):
        return (z + NZ - (k + 1) // 2) % NZ if k % 2 else (z + k // 2) % NZ

    relayed = []
    for t in range(1, HALF + 1):
        ways = (0, 1) if t < HALF else (0,)
        slots = (slot_at(2 * t - 1), slot_at(2 * t))
        for way in ways:
            own_copy(slots[way], way, t - 1).wait_recv()
            if t < HALF - way:
                own_copy(slots[way], way, t).start()
        for way in ways:
            for side in range(2):
                side_copy(slots[way], side, 2 * t - 1 + way).start()
        for piece in range(2):
            for way in ways:
                bundle_copy(slots[way], piece, way, t - 1).wait_recv()
                if t < HALF - way:
                    bundle_copy(slots[way], piece, way, t).start()
        ready = [0] if t == 1 else [2 * t - 3, 2 * t - 2]
        for k in ready:
            for side in range(2):
                side_copy(slot_at(k), side, k, arriving=True).wait_recv()
                relay_copy(slot_at(k), side, k).start()
        turn(t - 1)
    last = NZ - 1
    for side in range(2):
        side_copy(slot_at(last), side, last, arriving=True).wait_recv()
        relay_copy(slot_at(last), side, last).start()
    for k in range(NZ):
        for side in range(2):
            relay_copy(slot_at(k), side, k, arriving=True).wait_recv()

    acc = jnp.zeros((2 * BUS, NNET * SCN), F32)
    for j in range(NZ // 2):
        rows = gath[2 * j : 2 * j + 2].reshape(2 * BUS, NNET * SCN)
        acc = acc + jnp.dot(zt[j], rows, preferred_element_type=F32)
    vbuf[...] = acc.T.reshape(NX, NCORE, SCN, 2 * BUS)

    sib = n + 1 - 2 * c
    core_copy = remote(vbuf.at[:, 1 - c], cbuf, core_s, core_r, g, sib)
    core_copy.start()
    core_copy.wait_recv()
    wbuf[...] = vbuf[:, c] + cbuf[...]
    for d in range(1, NX):
        peer = (x + d) % NX
        remote(wbuf.at[peer], xbuf.at[x], x_s, x_r, g, peer * NCORE + c).start()
    xbuf[x] = wbuf[x]
    x_all = remote(wbuf.at[pl.ds(0, NX - 1)], xbuf.at[pl.ds(0, NX - 1)], x_s, x_r, g, n)
    x_all.wait_recv()
    volts = (xbuf[0] + xbuf[1]) + (xbuf[2] + xbuf[3])

    bus_lane = lane_iota((NGEN, BUS)) + 1
    back_hot = jnp.concatenate(
        [
            jnp.where(ids_in[:, r : r + 1].astype(jnp.int32) == bus_lane, 1.0, 0.0)
            for r in range(CAP)
        ],
        axis=0,
    ).astype(BF16)
    both = jnp.concatenate([volts[:, :BUS], volts[:, BUS:]], axis=0)
    for j, row in enumerate(pack(back_hot, both)):
        sback[:, j, :] = row
    sback[:, 3, :] = jnp.zeros((NGEN, 128), F32)

    def send_back(i, carry):
        peer = (g + i) % NGEN
        remote(sback.at[peer], rback.at[g], back_s, back_r, peer, n).start()
        return carry

    lax.fori_loop(1, NGEN, send_back, 0)
    rback[g] = sback[g]
    slot_hot = jnp.where(lane_iota((SLOTS, CAP * NGEN)) == code_s, 1.0, 0.0).astype(BF16)
    all_back = remote(
        sback.at[pl.ds(0, NGEN - 1)], rback.at[pl.ds(0, NGEN - 1)], back_s, back_r, g, n
    )
    all_back.wait_recv()
    at_gen = unpack(slot_hot, [rback[:, j, :] for j in range(3)]).T
    v_re, v_im = at_gen[:SCN], at_gen[SCN : 2 * SCN]

    sin_d, cos_d, emf_re, emf_im = keep[0], keep[1], keep[2], keep[3]
    omega, eq_t, eq_s, ed_s, efd = state[1], state[2], state[3], state[4], state[5]
    par = [params[k : k + 1, :] for k in range(13)]
    gen_re = (emf_im - v_im) / sub_x
    gen_im = (v_re - emf_re) / sub_x
    cur_d = gen_re * sin_d - gen_im * cos_d
    cur_q = gen_re * cos_d + gen_im * sin_d
    power = ed_s * cur_d + eq_s * cur_q
    term = jnp.sqrt(v_re * v_re + v_im * v_im + 0.01)
    out[0] = omega * active
    out[1] = (par[12] - power - par[1] * omega) / (2.0 * par[0]) * active
    out[2] = (efd - eq_t - (par[5] - par[6]) * cur_d) / par[2] * active
    out[3] = (eq_t - eq_s - (par[6] - sub_x) * cur_d) / par[3] * active
    out[4] = ((par[8] - sub_x) * cur_q - ed_s) / par[4] * active
    out[5] = (par[9] * (par[11] - term) - efd) / par[10] * active

    all_boxes.wait_send()
    all_msgs.wait_send()
    y_first.wait_send()
    for k in range(NZ):
        for side in range(2):
            side_copy(slot_at(k), side, k).wait_send()
            relay_copy(slot_at(k), side, k).wait_send()
    for t in range(HALF):
        for way in range(2):
            if t < HALF - way:
                own_copy(z, way, t).wait_send()
                for piece in range(2):
                    bundle_copy(z, piece, way, t).wait_send()
    core_copy.wait_send()
    x_all.wait_send()
    all_back.wait_send()


def body(state, params, gen_count, gen_block, gen_local, impedance, fault_bus, cleared, fault_volt):
    vmem = pl.BlockSpec(memory_space=pltpu.VMEM)
    dma = pltpu.SemaphoreType.DMA
    return pl.pallas_call(
        kernel,
        out_shape=jax.ShapeDtypeStruct(state.shape, F32),
        in_specs=[
            vmem,
            vmem,
            pl.BlockSpec(memory_space=pltpu.SMEM),
            vmem,
            vmem,
            pl.BlockSpec(memory_space=pl.ANY),
            vmem,
            vmem,
            vmem,
        ],
        out_specs=vmem,
        scratch_shapes=[
            pltpu.VMEM((2, NZ // 2, BUS, 2 * BUS), BF16),
            pltpu.VMEM((NZ // 2, 2 * BUS, 2 * BUS), BF16),
            pltpu.VMEM((NZ, NY, 3, 16, NNET * SCN), BF16),
            pltpu.VMEM((NGEN, 4, 128), F32),
            pltpu.VMEM((NGEN, 4, 128), F32),
            pltpu.VMEM((NNET, 16, 128), BF16),
            pltpu.VMEM((NNET, 16, 128), BF16),
            pltpu.VMEM((NX, NCORE, SCN, 2 * BUS), F32),
            pltpu.VMEM((NX, SCN, 2 * BUS), F32),
            pltpu.VMEM((NX, SCN, 2 * BUS), F32),
            pltpu.VMEM((NX, SCN, 2 * BUS), F32),
            pltpu.VMEM((NGEN, 4, 128), F32),
            pltpu.VMEM((NGEN, 4, 128), F32),
            pltpu.VMEM((4, SCN, SLOTS), F32),
            dma,
            dma,
            dma,
            dma,
            dma,
            dma,
            dma,
            dma((2, HALF)),
            dma((2, HALF)),
            dma((2, 2, HALF)),
            dma((2, 2, HALF)),
            dma((2, NZ)),
            dma((2, NZ)),
            dma((2, NZ)),
            dma((2, NZ)),
            dma,
            dma,
            dma,
            dma,
            dma,
            dma,
        ],
        compiler_params=pltpu.CompilerParams(
            collective_id=0, has_side_effects=True, vmem_limit_bytes=40 * 1024 * 1024
        ),
    )(
        state,
        params,
        gen_count,
        gen_block,
        gen_local.reshape(1, SLOTS),
        impedance.reshape(2, NZ // 2, BUS, 2 * BUS),
        fault_bus.reshape(1, SCN),
        cleared.reshape(1, SCN),
        fault_volt,
    )


def solution(mesh):
    in_specs = (
        P(None, "net", "gen"),
        P(None, "gen"),
        P("gen"),
        P("gen", None),
        P("gen"),
        P(None, "net", "gen"),
        P("net"),
        P("net"),
        P(None, "net"),
    )
    return jax.shard_map(
        body, mesh=mesh, in_specs=in_specs, out_specs=P(None, "net", "gen"), check_vma=False
    )
```

time: 467 us -> 97.5 us (0.21)
  waiting for transfers between devices: 390 us -> 0 us
  Pallas kernels: 0 us -> 89.1 us
  starting transfers between devices: 25.5 us -> 0 us
  between operations: 14 us -> 0.68 us
  blocking collectives: 11.7 us -> 0 us
  other arithmetic: 8.42 us -> 0 us
    all_gather x2 -> x0, waiting for transfers between devices: 290 us -> none  [the longest x1 171 us: body(): every_bus = lax.all_gather(volts, 'gen', axis=2, tiled=True)]
    pallas_call x0 -> x1, Pallas kernels: none -> 89.1 us  [body(): pl.pallas_call(kernel, out_shape=jax.ShapeDtypeStruct(state.shape, F32),...]
    psum x1 -> x0, waiting for transfers between devices: 79.5 us -> none  [body(): whole_volts = lax.psum(partial_volts, 'net')]
    all_to_all x2 -> x0, starting transfers between devices: 25.3 us -> none  [the longest x1 19.3 us: body(): lax.all_to_all(box_ids.reshape(n_cols, send_cap), 'gen', split_axis=0, co...]
    all_to_all x2 -> x0, waiting for transfers between devices: 20.9 us -> none  [the longest x1 12.4 us: body(): lax.all_to_all(box_cur.reshape(n_cols, send_cap, 2 * scen_dev), 'gen', sp...]
    all_to_all x1 -> x0, blocking collectives: 11.7 us -> none  [body(): lax.all_to_all(injected, 'net', split_axis=2, concat_axis=1, tiled=True)]
    unnamed x13 -> x16, local copies, waits for them, and re-layouts: 1.16 us -> 7.46 us
    gather x2 -> x0, local copies, waits for them, and re-layouts: 5.68 us -> none  [body(): at_gen = jnp.take(every_bus, bus_index, axis=2).transpose(1, 0, 2)]
  transfers between devices with their start and end apart: 5 -> 0, of which waited for: 5 -> 0; matrix products, arithmetic and copies ran while one was open for 1% -> 0% of each run, Pallas kernels for 0% -> 0%
where the time goes in v1:
time: 97.5 us; the launch traced here: 97.2 us
  Pallas kernels  89.1 us (91%)
  local copies, waits for them, and re-layouts  7.46 us (8%)
    pallas_call x1, Pallas kernels, body(): pl.pallas_call(kernel, out_shape=jax.ShapeDtypeStruct(state.shape, F32),...  89.1 us
    unnamed x16, local copies, waits for them, and re-layouts  7.46 us

profile of v1, /device:TPU:1, one launch (start us, length us, event | category | flops | bytes accessed | tf_op | source)
XLA Modules:
  0.0 97.2 jit_solution(14078807123727143273)
XLA Ops:
  0.7 0.8 copy.10.block
  1.5 0.0 copy-start
  1.5 1.7 %copy-done = bf16[2,1536,384]{2,1,0:T(8,128)(2,1)S(1)} copy-done((bf16[2,1536,384]{2,1,0:T(8,128)(2,1)S(1)}, bf16[2,1536,384]{2,1,0:T(8,128)(2,1)}, u32[]{:S(2)}) %copy-start) | copy-done | bytes 2359320
  3.1 0.0 copy-start.1
  3.1 0.9 copy-done.1
  4.1 0.0 copy-start.2
  4.1 0.7 copy-done.2
  4.8 0.0 copy-start.3
  4.8 0.7 copy-done.3
  5.5 0.0 copy-start.4
  5.5 0.7 copy-done.4
  6.1 0.0 copy-start.5
  6.1 0.7 copy-done.5
  6.8 0.0 copy-start.6
  6.8 0.7 copy-done.6
  7.5 89.1 %shard_map.91 = f32[6,32,256]{2,1,0:T(8,128)S(1)} custom-call(f32[6,32,256]{2,1,0:T(8,128)S(1)} %copy-done.1, f32[13,256]{1,0:T(8,128)S(1)} %copy-done.2, s32[1]{0:T(128)S(6)} %copy.12.count, s32[256,1]{1,0:T(8,128)S(1)} %copy.10.block, s32[1,256]{1,0:T(1,128)S(1)} %bitcast.5, bf16[2,8,192,384]{3,2,1,0:T(8,128)(2,1)S(1)} %bitcast.4, s32[1,32]{1,0:T(1,128)S(1)} %bitcast.6, ...), custom_call_target="tpu_custom_call" | custom-call | tf_op jit(solution)/shard_map/pallas_call | solution.py:413
  96.5 0.7 copy.13
Async XLA Ops:
  1.5 1.7 %copy-start = (bf16[2,1536,384]{2,1,0:T(8,128)(2,1)S(1)}, bf16[2,1536,384]{2,1,0:T(8,128)(2,1)}, u32[]{:S(2)}) copy-start(bf16[2,1536,384]{2,1,0:T(8,128)(2,1)} %param.14) | copy-start | bytes 7077892
  3.1 0.9 copy-start.1
  4.1 0.7 copy-start.2
  4.8 0.7 copy-start.3
  5.5 0.7 copy-start.4
  6.1 0.7 copy-start.5
  6.8 0.7 copy-start.6

commit v2 on v1

v2 whole, which is shorter than its diff:
```python
import functools

import jax
import jax.numpy as jnp
from jax import lax
from jax.experimental import pallas as pl
from jax.experimental.pallas import tpu as pltpu
from jax.sharding import PartitionSpec as P

F32 = jnp.float32
BF16 = jnp.bfloat16
NZ, NY, NX, NCORE = 16, 4, 4, 2
NGEN, NNET = NZ * NY, NX * NCORE
SCN = 32
SLOTS = 256
BUS = 192
SUB = BUS // NNET
CAP = 6
FAR = (0, NZ // 4, 3 * NZ // 4, NZ // 2)
BACK = (0, 2, 1, 3)
NT = (((1,), (1,)), ((), ()))


def remote(src, dst, send_sem, recv_sem, gen, net):
    return pltpu.make_async_remote_copy(
        src_ref=src,
        dst_ref=dst,
        send_sem=send_sem,
        recv_sem=recv_sem,
        device_id=(gen, net),
        device_id_type=pl.DeviceIdType.MESH,
    )


def three(v):
    hi = v.astype(BF16)
    rest = v - hi.astype(F32)
    mid = rest.astype(BF16)
    lo = (rest - mid.astype(F32)).astype(BF16)
    return hi, mid, lo


def lane_iota(shape):
    return lax.broadcasted_iota(jnp.int32, shape, len(shape) - 1)


def row_iota(shape):
    return lax.broadcasted_iota(jnp.int32, shape, 0)


def pack(hot, vals):
    hi, mid, lo = three(vals)
    rhs = jnp.concatenate([hi, mid, lo, lo], axis=0)
    out = lax.dot_general(hot, rhs, NT, preferred_element_type=F32)
    left, right = out[:, :128], out[:, 128:]
    both = left + pltpu.roll(left, 64, 1) + right
    low = lane_iota((NGEN, 128)) < 64
    rows = []
    for j in range(CAP // 2):
        even = both[2 * j * NGEN : (2 * j + 1) * NGEN]
        odd = both[(2 * j + 1) * NGEN : (2 * j + 2) * NGEN]
        rows.append(jnp.where(low, even, odd))
    return rows


def unpack(hot, rows):
    every = jnp.concatenate(rows, axis=0)
    turned = pltpu.roll(every, 64, 1)
    low = lane_iota(every.shape) < 64
    vals = jnp.concatenate([jnp.where(low, every, turned), jnp.where(low, turned, every)], axis=0)
    hi, mid, lo = three(vals)
    first = jnp.where(lane_iota(vals.shape) < 64, hi.astype(F32), mid.astype(F32)).astype(BF16)
    rhs = jnp.concatenate([first, lo], axis=1)
    out = jnp.dot(hot, rhs, preferred_element_type=F32)
    left, right = out[:, :128], out[:, 128:]
    return left + pltpu.roll(left, 64, 1) + right


def kernel(
    state_h,
    params_h,
    count_h,
    block_h,
    local_h,
    z_hbm,
    fbus_h,
    cleared_h,
    fvolt_h,
    out,
    state,
    params,
    count,
    block,
    local,
    zbuf,
    fbus,
    cleared,
    fvolt,
    zt,
    gath,
    sbox,
    rbox,
    smsg,
    rmsg,
    vbuf,
    cbuf,
    wbuf,
    xbuf,
    sback,
    rback,
    keep,
    back_hot,
    slot_hot,
    in_sem,
    box_s,
    box_r,
    msg_s,
    msg_r,
    near_s,
    near_r,
    side_s,
    side_r,
    core_s,
    core_r,
    x_s,
    x_r,
    back_s,
    back_r,
):
    g = lax.axis_index("gen")
    n = lax.axis_index("net")
    z, y = g // NY, g % NY
    x, c = n // NCORE, n % NCORE
    barrier = pltpu.get_barrier_semaphore()

    def peer_at(i):
        zi, yi = i // NY, i % NY
        dz = NZ + NZ // 2 + ((zi + 1) // 2) * (2 * (zi % 2) - 1)
        dy = 2 + yi + yi // 2 + 2 * (yi // 3)
        return ((z + dz) % NZ) * NY + (y + dy) % NY

    def greet(gen, net):
        pl.semaphore_signal(
            barrier, inc=1, device_id=(gen, net), device_id_type=pl.DeviceIdType.MESH
        )

    def greet_gen(i, carry):
        greet(peer_at(i), n)
        return carry

    lax.fori_loop(0, NGEN - 1, greet_gen, 0)
    for k in (3, 2, 1, 0):

        def greet_net(i, carry, far=FAR[k]):
            greet(((z + far) % NZ) * NY + y, (n + i) % NNET)
            return carry

        lax.fori_loop(1, NNET, greet_net, 0)

    loads = [
        pltpu.make_async_copy(src, dst, in_sem.at[i])
        for i, (src, dst) in enumerate(
            [
                (block_h, block),
                (state_h, state),
                (params_h, params),
                (count_h, count),
                (local_h, local),
                (fbus_h, fbus),
                (cleared_h, cleared),
                (fvolt_h, fvolt),
                (z_hbm, zbuf),
            ]
        )
    ]
    for load in loads:
        load.start()

    loads[0].wait()
    tgt_l = block[...].astype(F32)
    ii, jj = row_iota((SLOTS, SLOTS)), lane_iota((SLOTS, SLOTS))
    same = jnp.broadcast_to(tgt_l, (SLOTS, SLOTS)).T == tgt_l
    rank_l = jnp.sum(jnp.where(same & (ii < jj), 1.0, 0.0), axis=0, keepdims=True)
    send_hot = jnp.where(
        row_iota((CAP * NGEN, SLOTS)).astype(F32) == rank_l * NGEN + tgt_l, 1.0, 0.0
    ).astype(BF16)
    for load in loads[1:8]:
        load.wait()

    active = (lane_iota((1, SLOTS)) < count[0]).astype(F32)
    delta, eq_s, ed_s = state[0], state[3], state[4]
    sin_d = jnp.sin(delta)
    cos_d = jnp.cos(delta)
    emf_re = ed_s * sin_d + eq_s * cos_d
    emf_im = eq_s * sin_d - ed_s * cos_d
    keep[0] = sin_d
    keep[1] = cos_d
    keep[2] = emf_re
    keep[3] = emf_im
    sub_x = params[7:8, :]
    cur = jnp.concatenate([emf_im / sub_x * active, -emf_re / sub_x * active], axis=0)
    for j, row in enumerate(pack(send_hot, cur)):
        sbox[:, j, :] = row
    ids = lax.dot_general(
        send_hot,
        jnp.broadcast_to((local[...] + 1).astype(F32), (128, SLOTS)).astype(BF16),
        NT,
        preferred_element_type=F32,
    )
    lane = lane_iota((NGEN, 128))
    id_row = jnp.zeros((NGEN, 128), F32)
    for r in range(CAP):
        id_row = jnp.where(lane == r, ids[r * NGEN : (r + 1) * NGEN], id_row)
    sbox[:, 3, :] = id_row

    pl.semaphore_wait(barrier, NGEN - 1 + len(FAR) * (NNET - 1))

    def send_box(i, carry):
        peer = peer_at(i)
        remote(sbox.at[peer], rbox.at[g], box_s, box_r, peer, n).start()
        return carry

    lax.fori_loop(0, NGEN - 1, send_box, 0)
    rbox[g] = sbox[g]
    loads[8].wait()

    def turn(j):
        parts = [zbuf[p, j].astype(F32) for p in range(2)]
        rows = []
        for k in range(8):
            a = k * SUB
            rows += [
                parts[0][a : a + 16],
                parts[1][a : a + 16],
                parts[0][a + 16 : a + 24],
                parts[1][a + 16 : a + 24],
            ]
        zt[j] = jnp.concatenate(rows, axis=0).T.astype(BF16)

    for j in range(5):
        turn(j)
    half = (rank_l.astype(jnp.int32) % 2) * (3 * NGEN) + (rank_l.astype(jnp.int32) // 2) * NGEN
    code = half.astype(F32) + tgt_l
    code_s = jnp.broadcast_to(code, (128, SLOTS)).T
    slot_hot[...] = jnp.concatenate(
        [
            jnp.where((lane_iota((SLOTS, 128)) + 128 * k).astype(F32) == code_s, 1.0, 0.0)
            for k in range(3)
        ],
        axis=1,
    ).astype(BF16)
    row = row_iota((256, 1))
    part, i16 = (row % 128) // 16, row % 16
    bus = part * SUB + jnp.where(row < 128, i16, 16 + i16 % 8)
    fb, cl = fbus[...], cleared[...]
    fb4 = jnp.concatenate([fb] * 4, axis=1)
    on4 = 1.0 - jnp.concatenate([cl] * 4, axis=1).astype(F32)
    fv4 = jnp.concatenate([fvolt[0:1], fvolt[1:2]] * 2, axis=1)
    fault = 10.0 * fv4 * (jnp.where(bus + g * BUS == fb4, 1.0, 0.0) * on4)

    all_boxes = remote(
        sbox.at[pl.ds(0, NGEN - 1)], rbox.at[pl.ds(0, NGEN - 1)], box_s, box_r, g, n
    )
    all_boxes.wait_recv()

    ids_in = rbox[:, 3, :]
    ids_t = ids_in.T
    id_lane = jnp.concatenate([ids_t[r : r + 1] for r in (0, 2, 4, 1, 3, 5)], axis=1)
    bus_hot = jnp.where((bus + 1).astype(F32) == id_lane, 1.0, 0.0).astype(BF16)
    summed = unpack(bus_hot, [rbox[:, j, :] for j in range(3)])
    inject = summed - fault
    first, second = inject[:128], inject[128:]
    i16 = row_iota((128, 128)) % 16
    second = jnp.where(i16 < 8, second, pltpu.roll(second, 96, 1))
    message = jnp.where(lane_iota((128, 128)) < 64, first, second).astype(BF16)
    smsg[...] = message.reshape(NNET, 16, 128)

    for k in (3, 1, 2, 0):

        def send_msg(i, carry, k=k):
            peer = (n + i) % NNET
            gen = ((z + FAR[k]) % NZ) * NY + y
            remote(smsg.at[peer], rmsg.at[BACK[k], n], msg_s.at[k], msg_r.at[BACK[k]], gen, peer).start()
            return carry

        lax.fori_loop(0 if k else 1, NNET, send_msg, 0)
    rmsg[0, n] = smsg[n]

    def all_msgs(k):
        count = NNET if k else NNET - 1
        return remote(
            smsg.at[pl.ds(0, count)], rmsg.at[k, pl.ds(0, count)], msg_s.at[k], msg_r.at[k], g, n
        )

    near = (1, NZ - 1, 2)
    side = (1, NY - 1, 2)

    def near_copy(k, way):
        ref = gath.at[(z + FAR[k]) % NZ, y]
        return remote(
            ref, ref, near_s.at[way, k], near_r.at[way, k], ((z + near[way]) % NZ) * NY + y, n
        )

    def send_sides(slot):
        for d in side:
            ref = gath.at[slot, y]
            remote(ref, ref, side_s, side_r, z * NY + (y + d) % NY, n).start()

    def assemble(k):
        slot = (z + FAR[k]) % NZ
        all_msgs(k).wait_recv()
        tiles = [rmsg[k, m].astype(F32) for m in range(NNET)]
        for j in range(3):
            chunk = jnp.concatenate([t[:, SCN * j : SCN * (j + 1)] for t in tiles], axis=1)
            gath[slot, y, j] = chunk.astype(BF16)
        for way in (2, 0, 1):
            near_copy(k, way).start()
        send_sides(slot)

    def arrive(k):
        for way in range(3):
            near_copy(k, way).wait_recv()
            send_sides((z + FAR[k] + NZ - near[way]) % NZ)

    assemble(0)
    turn(5)
    assemble(1)
    assemble(2)
    turn(6)
    arrive(0)
    assemble(3)
    turn(7)
    bus_lane = lane_iota((NGEN, BUS)) + 1
    back_hot[...] = jnp.concatenate(
        [
            jnp.where(ids_in[:, r : r + 1].astype(jnp.int32) == bus_lane, 1.0, 0.0)
            for r in range(CAP)
        ],
        axis=0,
    ).astype(BF16)
    arrive(1)
    arrive(2)
    arrive(3)
    ref = gath.at[pl.ds(0, 3 * NZ // 4)]
    all_sides = remote(ref, ref, side_s, side_r, g, n)
    all_sides.wait_recv()

    acc = jnp.zeros((2 * BUS, NNET * SCN), F32)
    for j in range(NZ // 2):
        rows = gath[2 * j : 2 * j + 2].reshape(2 * BUS, NNET * SCN)
        acc = acc + jnp.dot(zt[j], rows, preferred_element_type=F32)
    vbuf[...] = acc.T.reshape(NX, NCORE, SCN, 2 * BUS)

    sib = n + 1 - 2 * c
    core_copy = remote(vbuf.at[:, 1 - c], cbuf, core_s, core_r, g, sib)
    core_copy.start()
    core_copy.wait_recv()
    wbuf[...] = vbuf[:, c] + cbuf[...]
    for d in (2, 1, 3):
        peer = (x + d) % NX
        remote(wbuf.at[peer], xbuf.at[x], x_s, x_r, g, peer * NCORE + c).start()
    xbuf[x] = wbuf[x]
    x_all = remote(wbuf.at[pl.ds(0, NX - 1)], xbuf.at[pl.ds(0, NX - 1)], x_s, x_r, g, n)
    x_all.wait_recv()
    volts = (xbuf[0] + xbuf[1]) + (xbuf[2] + xbuf[3])

    both = jnp.concatenate([volts[:, :BUS], volts[:, BUS:]], axis=0)
    for j, row in enumerate(pack(back_hot[...], both)):
        sback[:, j, :] = row

    def send_back(i, carry):
        peer = peer_at(i)
        remote(
            sback.at[peer, pl.ds(0, 3)], rback.at[g, pl.ds(0, 3)], back_s, back_r, peer, n
        ).start()
        return carry

    lax.fori_loop(0, NGEN - 1, send_back, 0)
    rback[g, 0:3] = sback[g, 0:3]

    all_boxes.wait_send()
    for k in range(4):
        all_msgs(k).wait_send()
        for way in range(3):
            near_copy(k, way).wait_send()
    all_sides.wait_send()
    core_copy.wait_send()
    x_all.wait_send()

    all_back = remote(
        sback.at[pl.ds(0, NGEN - 1), pl.ds(0, 3)],
        rback.at[pl.ds(0, NGEN - 1), pl.ds(0, 3)],
        back_s,
        back_r,
        g,
        n,
    )
    all_back.wait_recv()
    at_gen = unpack(slot_hot[...], [rback[:, j, :] for j in range(3)]).T
    v_re, v_im = at_gen[:SCN], at_gen[SCN : 2 * SCN]

    sin_d, cos_d, emf_re, emf_im = keep[0], keep[1], keep[2], keep[3]
    omega, eq_t, eq_s, ed_s, efd = state[1], state[2], state[3], state[4], state[5]
    par = [params[k : k + 1, :] for k in range(13)]
    gen_re = (emf_im - v_im) / sub_x
    gen_im = (v_re - emf_re) / sub_x
    cur_d = gen_re * sin_d - gen_im * cos_d
    cur_q = gen_re * cos_d + gen_im * sin_d
    power = ed_s * cur_d + eq_s * cur_q
    term = jnp.sqrt(v_re * v_re + v_im * v_im + 0.01)
    out[0] = omega * active
    out[1] = (par[12] - power - par[1] * omega) / (2.0 * par[0]) * active
    out[2] = (efd - eq_t - (par[5] - par[6]) * cur_d) / par[2] * active
    out[3] = (eq_t - eq_s - (par[6] - sub_x) * cur_d) / par[3] * active
    out[4] = ((par[8] - sub_x) * cur_q - ed_s) / par[4] * active
    out[5] = (par[9] * (par[11] - term) - efd) / par[10] * active

    all_back.wait_send()


def body(state, params, gen_count, gen_block, gen_local, impedance, fault_bus, cleared, fault_volt):
    dma = pltpu.SemaphoreType.DMA
    inputs = (
        state,
        params,
        gen_count,
        gen_block.reshape(1, SLOTS),
        gen_local.reshape(1, SLOTS),
        impedance.reshape(2, NZ // 2, BUS, 2 * BUS),
        fault_bus.reshape(1, SCN),
        cleared.reshape(1, SCN),
        fault_volt,
    )
    return pl.pallas_call(
        kernel,
        out_shape=jax.ShapeDtypeStruct(state.shape, F32),
        in_specs=[pl.BlockSpec(memory_space=pltpu.HBM)] * len(inputs),
        out_specs=pl.BlockSpec(memory_space=pltpu.VMEM),
        scratch_shapes=[
            (pltpu.SMEM if v.ndim == 1 else pltpu.VMEM)(v.shape, v.dtype) for v in inputs
        ]
        + [
            pltpu.VMEM((NZ // 2, 2 * BUS, 2 * BUS), BF16),
            pltpu.VMEM((NZ, NY, 3, 16, NNET * SCN), BF16),
            pltpu.VMEM((NGEN, 4, 128), F32),
            pltpu.VMEM((NGEN, 4, 128), F32),
            pltpu.VMEM((NNET, 16, 128), BF16),
            pltpu.VMEM((4, NNET, 16, 128), BF16),
            pltpu.VMEM((NX, NCORE, SCN, 2 * BUS), F32),
            pltpu.VMEM((NX, SCN, 2 * BUS), F32),
            pltpu.VMEM((NX, SCN, 2 * BUS), F32),
            pltpu.VMEM((NX, SCN, 2 * BUS), F32),
            pltpu.VMEM((NGEN, 4, 128), F32),
            pltpu.VMEM((NGEN, 4, 128), F32),
            pltpu.VMEM((4, SCN, SLOTS), F32),
            pltpu.VMEM((CAP * NGEN, BUS), BF16),
            pltpu.VMEM((SLOTS, CAP * NGEN), BF16),
            dma((9,)),
            dma,
            dma,
            dma((4,)),
            dma((4,)),
            dma((3, 4)),
            dma((3, 4)),
            dma,
            dma,
            dma,
            dma,
            dma,
            dma,
            dma,
            dma,
        ],
        compiler_params=pltpu.CompilerParams(
            collective_id=0, has_side_effects=True, vmem_limit_bytes=64 * 1024 * 1024 - 65536
        ),
    )(*inputs)


def solution(mesh):
    in_specs = (
        P(None, "net", "gen"),
        P(None, "gen"),
        P("gen"),
        P("gen", None),
        P("gen"),
        P(None, "net", "gen"),
        P("net"),
        P("net"),
        P(None, "net"),
    )
    return jax.shard_map(
        body, mesh=mesh, in_specs=in_specs, out_specs=P(None, "net", "gen"), check_vma=False
    )
```

time: 97.5 us -> 79.6 us (0.82)
  Pallas kernels: 89.1 us -> 77.2 us
  local copies, waits for them, and re-layouts: 7.46 us -> 1.62 us
    pallas_call x1, Pallas kernels: 89.1 us -> 77.2 us  [body(): pl.pallas_call(kernel, out_shape=jax.ShapeDtypeStruct(state.shape, F32),...]
    unnamed x16 -> x1, local copies, waits for them, and re-layouts: 7.46 us -> 1.62 us
where the time goes in v2:
time: 79.6 us; the launch traced here: 79.5 us
  Pallas kernels  77.2 us (97%)
  local copies, waits for them, and re-layouts  1.62 us (2%)
    pallas_call x1, Pallas kernels, body(): pl.pallas_call(kernel, out_shape=jax.ShapeDtypeStruct(state.shape, F32),...  77.2 us
    unnamed x1, local copies, waits for them, and re-layouts  1.62 us

profile of v2, /device:TPU:1, one launch (start us, length us, event | category | flops | bytes accessed | tf_op | source)
XLA Modules:
  0.0 79.5 jit_solution(14743882874734631144)
XLA Ops:
  0.7 77.2 %shard_map.91 = f32[6,32,256]{2,1,0:T(8,128)} custom-call(f32[6,32,256]{2,1,0:T(8,128)} %state_h.1, f32[13,256]{1,0:T(8,128)} %params_h.1, s32[1]{0:T(128)S(6)} %copy.11.count_h, s32[1,256]{1,0:T(1,128)} %bitcast.6, s32[1,256]{1,0:T(1,128)} %bitcast.7, bf16[2,8,192,384]{3,2,1,0:T(8,128)(2,1)} %bitcast.5, s32[1,32]{1,0:T(1,128)} %bitcast.8, s32[1,32]{1,0:T(1,128)} %bitcast.9, ...), custom_call_target="tpu_custom_call" | custom-call | tf_op jit(solution)/shard_map/pallas_call | solution.py:434
  77.9 1.6 %copy.12 = f32[6,32,256]{2,1,0:T(8,128)} copy(f32[6,32,256]{2,1,0:T(8,128)} %shard_map.91) | data formatting | bytes 393216

commit v3 on v2

--- a/solution.py
+++ b/solution.py
@@ -16,8 +16,11 @@
 BUS = 192
 SUB = BUS // NNET
 CAP = 6
-FAR = (0, NZ // 4, 3 * NZ // 4, NZ // 2)
+FAR = (0, 5, NZ - 5, NZ // 2)
 BACK = (0, 2, 1, 3)
+NEAR = (1, NZ - 1, 2, NZ - 2)
+SIDE = (1, NY - 1, 2)
+TILE = 128
 NT = (((1,), (1,)), ((), ()))
 
 
@@ -148,14 +151,12 @@
         greet(peer_at(i), n)
         return carry
 
+    def greet_net(i, carry):
+        greet(g, (n + i) % NNET)
+        return carry
+
     lax.fori_loop(0, NGEN - 1, greet_gen, 0)
-    for k in (3, 2, 1, 0):
-
-        def greet_net(i, carry, far=FAR[k]):
-            greet(((z + far) % NZ) * NY + y, (n + i) % NNET)
-            return carry
-
-        lax.fori_loop(1, NNET, greet_net, 0)
+    lax.fori_loop(1, NNET, greet_net, 0)
 
     loads = [
         pltpu.make_async_copy(src, dst, in_sem.at[i])
@@ -213,7 +214,7 @@
         id_row = jnp.where(lane == r, ids[r * NGEN : (r + 1) * NGEN], id_row)
     sbox[:, 3, :] = id_row
 
-    pl.semaphore_wait(barrier, NGEN - 1 + len(FAR) * (NNET - 1))
+    pl.semaphore_wait(barrier, NGEN - 1 + NNET - 1)
 
     def send_box(i, carry):
         peer = peer_at(i)
@@ -275,7 +276,7 @@
     message = jnp.where(lane_iota((128, 128)) < 64, first, second).astype(BF16)
     smsg[...] = message.reshape(NNET, 16, 128)
 
-    for k in (3, 1, 2, 0):
+    for k in (0, 1, 2, 3):
 
         def send_msg(i, carry, k=k):
             peer = (n + i) % NNET
@@ -292,17 +293,14 @@
             smsg.at[pl.ds(0, count)], rmsg.at[k, pl.ds(0, count)], msg_s.at[k], msg_r.at[k], g, n
         )
 
-    near = (1, NZ - 1, 2)
-    side = (1, NY - 1, 2)
-
     def near_copy(k, way):
         ref = gath.at[(z + FAR[k]) % NZ, y]
         return remote(
-            ref, ref, near_s.at[way, k], near_r.at[way, k], ((z + near[way]) % NZ) * NY + y, n
+            ref, ref, near_s.at[way, k], near_r.at[way, k], ((z + NEAR[way]) % NZ) * NY + y, n
         )
 
     def send_sides(slot):
-        for d in side:
+        for d in SIDE:
             ref = gath.at[slot, y]
             remote(ref, ref, side_s, side_r, z * NY + (y + d) % NY, n).start()
 
@@ -313,14 +311,15 @@
         for j in range(3):
             chunk = jnp.concatenate([t[:, SCN * j : SCN * (j + 1)] for t in tiles], axis=1)
             gath[slot, y, j] = chunk.astype(BF16)
-        for way in (2, 0, 1):
-            near_copy(k, way).start()
+        if k < 3:
+            for way in (2, 3, 0, 1):
+                near_copy(k, way).start()
         send_sides(slot)
 
     def arrive(k):
-        for way in range(3):
+        for way in range(4):
             near_copy(k, way).wait_recv()
-            send_sides((z + FAR[k] + NZ - near[way]) % NZ)
+            send_sides((z + FAR[k] + NZ - NEAR[way]) % NZ)
 
     assemble(0)
     turn(5)
@@ -340,29 +339,56 @@
     ).astype(BF16)
     arrive(1)
     arrive(2)
-    arrive(3)
     ref = gath.at[pl.ds(0, 3 * NZ // 4)]
     all_sides = remote(ref, ref, side_s, side_r, g, n)
     all_sides.wait_recv()
 
-    acc = jnp.zeros((2 * BUS, NNET * SCN), F32)
-    for j in range(NZ // 2):
-        rows = gath[2 * j : 2 * j + 2].reshape(2 * BUS, NNET * SCN)
-        acc = acc + jnp.dot(zt[j], rows, preferred_element_type=F32)
-    vbuf[...] = acc.T.reshape(NX, NCORE, SCN, 2 * BUS)
-
     sib = n + 1 - 2 * c
-    core_copy = remote(vbuf.at[:, 1 - c], cbuf, core_s, core_r, g, sib)
-    core_copy.start()
-    core_copy.wait_recv()
-    wbuf[...] = vbuf[:, c] + cbuf[...]
-    for d in (2, 1, 3):
-        peer = (x + d) % NX
-        remote(wbuf.at[peer], xbuf.at[x], x_s, x_r, g, peer * NCORE + c).start()
-    xbuf[x] = wbuf[x]
-    x_all = remote(wbuf.at[pl.ds(0, NX - 1)], xbuf.at[pl.ds(0, NX - 1)], x_s, x_r, g, n)
-    x_all.wait_recv()
-    volts = (xbuf[0] + xbuf[1]) + (xbuf[2] + xbuf[3])
+    tiles = range(2 * BUS // TILE)
+
+    def core_copy(q):
+        return remote(vbuf.at[q, :, 1 - c], cbuf.at[q], core_s.at[q], core_r.at[q], g, sib)
+
+    def x_all(q):
+        return remote(
+            wbuf.at[q, pl.ds(0, NX - 1)],
+            xbuf.at[q, pl.ds(0, NX - 1)],
+            x_s.at[q],
+            x_r.at[q],
+            g,
+            n,
+        )
+
+    def product(q):
+        acc = jnp.zeros((TILE, NNET * SCN), F32)
+        for j in range(NZ // 2):
+            rows = gath[2 * j : 2 * j + 2].reshape(2 * BUS, NNET * SCN)
+            acc = acc + jnp.dot(
+                zt[j, TILE * q : TILE * (q + 1)], rows, preferred_element_type=F32
+            )
+        vbuf[q] = acc.T.reshape(NX, NCORE, SCN, TILE)
+        core_copy(q).start()
+
+    def add_core(q):
+        core_copy(q).wait_recv()
+        wbuf[q] = vbuf[q, :, c] + cbuf[q]
+        for d in (2, 1, 3):
+            peer = (x + d) % NX
+            remote(
+                wbuf.at[q, peer], xbuf.at[q, x], x_s.at[q], x_r.at[q], g, peer * NCORE + c
+            ).start()
+        xbuf[q, x] = wbuf[q, x]
+
+    for q in tiles:
+        product(q)
+        if q:
+            add_core(q - 1)
+    add_core(tiles[-1])
+    volts = []
+    for q in tiles:
+        x_all(q).wait_recv()
+        volts.append((xbuf[q, 0] + xbuf[q, 1]) + (xbuf[q, 2] + xbuf[q, 3]))
+    volts = jnp.concatenate(volts, axis=1)
 
     both = jnp.concatenate([volts[:, :BUS], volts[:, BUS:]], axis=0)
     for j, row in enumerate(pack(back_hot[...], both)):
@@ -381,11 +407,13 @@
     all_boxes.wait_send()
     for k in range(4):
         all_msgs(k).wait_send()
-        for way in range(3):
-            near_copy(k, way).wait_send()
+        if k < 3:
+            for way in range(4):
+                near_copy(k, way).wait_send()
     all_sides.wait_send()
-    core_copy.wait_send()
-    x_all.wait_send()
+    for q in tiles:
+        core_copy(q).wait_send()
+        x_all(q).wait_send()
 
     all_back = remote(
         sback.at[pl.ds(0, NGEN - 1), pl.ds(0, 3)],
@@ -446,10 +474,10 @@
             pltpu.VMEM((NGEN, 4, 128), F32),
             pltpu.VMEM((NNET, 16, 128), BF16),
             pltpu.VMEM((4, NNET, 16, 128), BF16),
-            pltpu.VMEM((NX, NCORE, SCN, 2 * BUS), F32),
-            pltpu.VMEM((NX, SCN, 2 * BUS), F32),
-            pltpu.VMEM((NX, SCN, 2 * BUS), F32),
-            pltpu.VMEM((NX, SCN, 2 * BUS), F32),
+            pltpu.VMEM((2 * BUS // TILE, NX, NCORE, SCN, TILE), F32),
+            pltpu.VMEM((2 * BUS // TILE, NX, SCN, TILE), F32),
+            pltpu.VMEM((2 * BUS // TILE, NX, SCN, TILE), F32),
+            pltpu.VMEM((2 * BUS // TILE, NX, SCN, TILE), F32),
             pltpu.VMEM((NGEN, 4, 128), F32),
             pltpu.VMEM((NGEN, 4, 128), F32),
             pltpu.VMEM((4, SCN, SLOTS), F32),
@@ -460,14 +488,14 @@
             dma,
             dma((4,)),
             dma((4,)),
-            dma((3, 4)),
-            dma((3, 4)),
+            dma((4, 3)),
+            dma((4, 3)),
             dma,
             dma,
-            dma,
-            dma,
-            dma,
-            dma,
+            dma((2 * BUS // TILE,)),
+            dma((2 * BUS // TILE,)),
+            dma((2 * BUS // TILE,)),
+            dma((2 * BUS // TILE,)),
             dma,
             dma,
         ],

time: 79.6 us -> 75.3 us (0.946)
  Pallas kernels: 77.2 us -> 72.9 us
    pallas_call x1, Pallas kernels: 77.2 us -> 72.9 us  [body(): pl.pallas_call(kernel, out_shape=jax.ShapeDtypeStruct(state.shape, F32),...]
where the time goes in v3:
time: 75.3 us; the launch traced here: 75.1 us
  Pallas kernels  72.9 us (97%)
  local copies, waits for them, and re-layouts  1.62 us (2%)
    pallas_call x1, Pallas kernels, body(): pl.pallas_call(kernel, out_shape=jax.ShapeDtypeStruct(state.shape, F32),...  72.9 us
    unnamed x1, local copies, waits for them, and re-layouts  1.62 us

profile of v3, /device:TPU:1, one launch (start us, length us, event | category | flops | bytes accessed | tf_op | source)
XLA Modules:
  0.0 75.1 jit_solution(1789182271890629112)
XLA Ops:
  0.7 72.9 %shard_map.91 = f32[6,32,256]{2,1,0:T(8,128)} custom-call(f32[6,32,256]{2,1,0:T(8,128)} %state_h.1, f32[13,256]{1,0:T(8,128)} %params_h.1, s32[1]{0:T(128)S(6)} %copy.11.count_h, s32[1,256]{1,0:T(1,128)} %bitcast.6, s32[1,256]{1,0:T(1,128)} %bitcast.7, bf16[2,8,192,384]{3,2,1,0:T(8,128)(2,1)} %bitcast.5, s32[1,32]{1,0:T(1,128)} %bitcast.8, s32[1,32]{1,0:T(1,128)} %bitcast.9, ...), custom_call_target="tpu_custom_call" | custom-call | tf_op jit(solution)/shard_map/pallas_call | solution.py:462
  73.5 1.6 %copy.12 = f32[6,32,256]{2,1,0:T(8,128)} copy(f32[6,32,256]{2,1,0:T(8,128)} %shard_map.91) | data formatting | bytes 393216

commit v4 on v3

--- a/solution.py
+++ b/solution.py
@@ -20,6 +20,7 @@
 BACK = (0, 2, 1, 3)
 NEAR = (1, NZ - 1, 2, NZ - 2)
 SIDE = (1, NY - 1, 2)
+RELAY = 8
 TILE = 128
 NT = (((1,), (1,)), ((), ()))
 
@@ -114,6 +115,7 @@
     keep,
     back_hot,
     slot_hot,
+    acc,
     in_sem,
     box_s,
     box_r,
@@ -121,8 +123,14 @@
     msg_r,
     near_s,
     near_r,
+    bundle_s,
+    bundle_r,
+    early_s,
+    early_r,
     side_s,
     side_r,
+    relay_s,
+    relay_r,
     core_s,
     core_r,
     x_s,
@@ -236,7 +244,9 @@
                 parts[0][a + 16 : a + 24],
                 parts[1][a + 16 : a + 24],
             ]
-        zt[j] = jnp.concatenate(rows, axis=0).T.astype(BF16)
+        turned = jnp.concatenate(rows, axis=0).T.astype(BF16)
+        zt[2 * j] = turned[:, :BUS]
+        zt[2 * j + 1] = turned[:, BUS:]
 
     for j in range(5):
         turn(j)
@@ -293,41 +303,95 @@
             smsg.at[pl.ds(0, count)], rmsg.at[k, pl.ds(0, count)], msg_s.at[k], msg_r.at[k], g, n
         )
 
+    slots = [(z + FAR[k]) % NZ for k in range(3)]
+    for k in (0, 3, 1, 2):
+        if k == 3:
+            slots.append((z + FAR[3]) % NZ)
+        else:
+            slots += [(z + FAR[k] + NZ - d) % NZ for d in NEAR]
+    first = (0, 1, 2, 7)
+    after = (3, 8, 12)
+
     def near_copy(k, way):
-        ref = gath.at[(z + FAR[k]) % NZ, y]
-        return remote(
-            ref, ref, near_s.at[way, k], near_r.at[way, k], ((z + NEAR[way]) % NZ) * NY + y, n
-        )
-
-    def send_sides(slot):
-        for d in SIDE:
-            ref = gath.at[slot, y]
-            remote(ref, ref, side_s, side_r, z * NY + (y + d) % NY, n).start()
+        ref = gath.at[slots[k], y, pl.ds(1, 2)]
+        gen = ((z + NEAR[way]) % NZ) * NY + y
+        return remote(ref, ref, near_s.at[way, k], near_r.at[way, k], gen, n)
+
+    def bundle_copy(k, way):
+        ref = gath.at[slots[k], :, 0]
+        gen = ((z + NEAR[way]) % NZ) * NY + y
+        return remote(ref, ref, bundle_s.at[way, k], bundle_r.at[way, k], gen, n)
+
+    def early_copy(k, way):
+        ref = gath.at[slots[first[k]], y, 0]
+        gen = z * NY + (y + SIDE[way]) % NY
+        return remote(ref, ref, early_s.at[way, k], early_r.at[way, k], gen, n)
+
+    def side_copy(m, way):
+        ref = gath.at[slots[m], y, pl.ds(1, 2)]
+        gen = z * NY + (y + SIDE[way]) % NY
+        return remote(ref, ref, side_s.at[way, m], side_r.at[way, m], gen, n)
+
+    def relay_copy(m, way):
+        ref = gath.at[slots[m], (y + SIDE[1 - way]) % NY, 1 + way]
+        gen = z * NY + (y + SIDE[way]) % NY
+        return remote(ref, ref, relay_s.at[way, m], relay_r.at[way, m], gen, n)
+
+    def send_sides(m):
+        for way in range(2 if m < RELAY else 3):
+            side_copy(m, way).start()
+
+    def relay(m):
+        for way in range(2):
+            side_copy(m, way).wait_recv()
+            relay_copy(m, way).start()
 
     def assemble(k):
-        slot = (z + FAR[k]) % NZ
         all_msgs(k).wait_recv()
         tiles = [rmsg[k, m].astype(F32) for m in range(NNET)]
         for j in range(3):
             chunk = jnp.concatenate([t[:, SCN * j : SCN * (j + 1)] for t in tiles], axis=1)
-            gath[slot, y, j] = chunk.astype(BF16)
+            gath[slots[first[k]], y, j] = chunk.astype(BF16)
+        for way in (2, 0, 1):
+            early_copy(k, way).start()
         if k < 3:
             for way in (2, 3, 0, 1):
                 near_copy(k, way).start()
-        send_sides(slot)
-
-    def arrive(k):
-        for way in range(4):
-            near_copy(k, way).wait_recv()
-            send_sides((z + FAR[k] + NZ - NEAR[way]) % NZ)
+        send_sides(first[k])
+
+    def bundle(k):
+        for way in range(3):
+            early_copy(k, way).wait_recv()
+        if k < 3:
+            for way in (2, 3, 0, 1):
+                bundle_copy(k, way).start()
+
+    def arrive(k, way):
+        near_copy(k, way).wait_recv()
+        send_sides(after[k] + way)
 
     assemble(0)
     turn(5)
+    for way in range(2):
+        arrive(0, way)
+    bundle(0)
+    for way in range(2, 4):
+        arrive(0, way)
+    relay(0)
     assemble(1)
     assemble(2)
+    assemble(3)
     turn(6)
-    arrive(0)
-    assemble(3)
+    for m in (3, 4, 5, 6):
+        relay(m)
+    bundle(1)
+    bundle(2)
+    for way in range(4):
+        arrive(1, way)
+        if way < 3:
+            relay((1, 2, 7)[way])
+    for way in range(4):
+        arrive(2, way)
     turn(7)
     bus_lane = lane_iota((NGEN, BUS)) + 1
     back_hot[...] = jnp.concatenate(
@@ -337,11 +401,31 @@
         ],
         axis=0,
     ).astype(BF16)
-    arrive(1)
-    arrive(2)
-    ref = gath.at[pl.ds(0, 3 * NZ // 4)]
-    all_sides = remote(ref, ref, side_s, side_r, g, n)
-    all_sides.wait_recv()
+    bundle(3)
+
+    def product(group, rows=slice(None)):
+        total = None
+        for m in group:
+            part = jnp.dot(
+                zt[slots[m], rows],
+                gath[slots[m]].reshape(BUS, NNET * SCN),
+                preferred_element_type=F32,
+            )
+            total = part if total is None else total + part
+        return total
+
+    groups = (range(0, 4), range(4, 8), range(8, 12), range(12, 16))
+    for i, group in enumerate(groups):
+        for m in group:
+            for way in range(2 if m < RELAY else 3):
+                (relay_copy if m < RELAY else side_copy)(m, way).wait_recv()
+            for k in range(3):
+                if after[k] <= m < after[k] + 4:
+                    bundle_copy(k, m - after[k]).wait_recv()
+        if i == 0:
+            acc[...] = product(group)
+        elif i < 3:
+            acc[...] += product(group)
 
     sib = n + 1 - 2 * c
     tiles = range(2 * BUS // TILE)
@@ -359,14 +443,10 @@
             n,
         )
 
-    def product(q):
-        acc = jnp.zeros((TILE, NNET * SCN), F32)
-        for j in range(NZ // 2):
-            rows = gath[2 * j : 2 * j + 2].reshape(2 * BUS, NNET * SCN)
-            acc = acc + jnp.dot(
-                zt[j, TILE * q : TILE * (q + 1)], rows, preferred_element_type=F32
-            )
-        vbuf[q] = acc.T.reshape(NX, NCORE, SCN, TILE)
+    def finish(q):
+        rows = slice(TILE * q, TILE * (q + 1))
+        whole = acc[rows] + product(groups[3], rows)
+        vbuf[q] = whole.T.reshape(NX, NCORE, SCN, TILE)
         core_copy(q).start()
 
     def add_core(q):
@@ -380,7 +460,7 @@
         xbuf[q, x] = wbuf[q, x]
 
     for q in tiles:
-        product(q)
+        finish(q)
         if q:
             add_core(q - 1)
     add_core(tiles[-1])
@@ -407,10 +487,17 @@
     all_boxes.wait_send()
     for k in range(4):
         all_msgs(k).wait_send()
+        for way in range(3):
+            early_copy(k, way).wait_send()
         if k < 3:
             for way in range(4):
                 near_copy(k, way).wait_send()
-    all_sides.wait_send()
+                bundle_copy(k, way).wait_send()
+    for m in range(NZ):
+        for way in range(2 if m < RELAY else 3):
+            side_copy(m, way).wait_send()
+            if m < RELAY:
+                relay_copy(m, way).wait_send()
     for q in tiles:
         core_copy(q).wait_send()
         x_all(q).wait_send()
@@ -468,7 +555,7 @@
             (pltpu.SMEM if v.ndim == 1 else pltpu.VMEM)(v.shape, v.dtype) for v in inputs
         ]
         + [
-            pltpu.VMEM((NZ // 2, 2 * BUS, 2 * BUS), BF16),
+            pltpu.VMEM((NZ, 2 * BUS, BUS), BF16),
             pltpu.VMEM((NZ, NY, 3, 16, NNET * SCN), BF16),
             pltpu.VMEM((NGEN, 4, 128), F32),
             pltpu.VMEM((NGEN, 4, 128), F32),
@@ -483,6 +570,7 @@
             pltpu.VMEM((4, SCN, SLOTS), F32),
             pltpu.VMEM((CAP * NGEN, BUS), BF16),
             pltpu.VMEM((SLOTS, CAP * NGEN), BF16),
+            pltpu.VMEM((2 * BUS, NNET * SCN), F32),
             dma((9,)),
             dma,
             dma,
@@ -490,8 +578,14 @@
             dma((4,)),
             dma((4, 3)),
             dma((4, 3)),
-            dma,
-            dma,
+            dma((4, 3)),
+            dma((4, 3)),
+            dma((3, 4)),
+            dma((3, 4)),
+            dma((3, NZ)),
+            dma((3, NZ)),
+            dma((2, RELAY)),
+            dma((2, RELAY)),
             dma((2 * BUS // TILE,)),
             dma((2 * BUS // TILE,)),
             dma((2 * BUS // TILE,)),

time: 75.3 us -> 70.4 us (0.935)
  Pallas kernels: 72.9 us -> 68 us
    pallas_call x1, Pallas kernels: 72.9 us -> 68 us  [body(): pl.pallas_call(kernel, out_shape=jax.ShapeDtypeStruct(state.shape, F32),...]
where the time goes in v4:
time: 70.4 us; the launch traced here: 70.3 us
  Pallas kernels  68 us (97%)
  local copies, waits for them, and re-layouts  1.62 us (2%)
    pallas_call x1, Pallas kernels, body(): pl.pallas_call(kernel, out_shape=jax.ShapeDtypeStruct(state.shape, F32),...  68 us
    unnamed x1, local copies, waits for them, and re-layouts  1.62 us

profile of v4, /device:TPU:1, one launch (start us, length us, event | category | flops | bytes accessed | tf_op | source)
XLA Modules:
  0.0 70.3 jit_solution(3113927404246165892)
XLA Ops:
  0.7 68.0 %shard_map.91 = f32[6,32,256]{2,1,0:T(8,128)} custom-call(f32[6,32,256]{2,1,0:T(8,128)} %state_h.1, f32[13,256]{1,0:T(8,128)} %params_h.1, s32[1]{0:T(128)S(6)} %copy.11.count_h, s32[1,256]{1,0:T(1,128)} %bitcast.6, s32[1,256]{1,0:T(1,128)} %bitcast.7, bf16[2,8,192,384]{3,2,1,0:T(8,128)(2,1)} %bitcast.5, s32[1,32]{1,0:T(1,128)} %bitcast.8, s32[1,32]{1,0:T(1,128)} %bitcast.9, ...), custom_call_target="tpu_custom_call" | custom-call | tf_op jit(solution)/shard_map/pallas_call | solution.py:549
  68.6 1.6 %copy.12 = f32[6,32,256]{2,1,0:T(8,128)} copy(f32[6,32,256]{2,1,0:T(8,128)} %shard_map.91) | data formatting | bytes 393216

commit v5 on v4

--- a/solution.py
+++ b/solution.py
@@ -20,7 +20,8 @@
 BACK = (0, 2, 1, 3)
 NEAR = (1, NZ - 1, 2, NZ - 2)
 SIDE = (1, NY - 1, 2)
-RELAY = 8
+EARLY = (1, 2, 1, 1)
+RELAY = (0, 3, 4, 5, 6, 7)
 TILE = 128
 NT = (((1,), (1,)), ((), ()))
 
@@ -309,26 +310,30 @@
             slots.append((z + FAR[3]) % NZ)
         else:
             slots += [(z + FAR[k] + NZ - d) % NZ for d in NEAR]
-    first = (0, 1, 2, 7)
+    origin = (0, 1, 2, 7)
+    source = (0, 1, 2, 0, 0, 0, 0, 3, 1, 1, 1, 1, 2, 2, 2, 2)
     after = (3, 8, 12)
 
+    def late(k):
+        return pl.ds(EARLY[k], 3 - EARLY[k])
+
     def near_copy(k, way):
-        ref = gath.at[slots[k], y, pl.ds(1, 2)]
+        ref = gath.at[slots[k], y, late(k)]
         gen = ((z + NEAR[way]) % NZ) * NY + y
         return remote(ref, ref, near_s.at[way, k], near_r.at[way, k], gen, n)
 
     def bundle_copy(k, way):
-        ref = gath.at[slots[k], :, 0]
+        ref = gath.at[slots[k], :, pl.ds(0, EARLY[k])]
         gen = ((z + NEAR[way]) % NZ) * NY + y
         return remote(ref, ref, bundle_s.at[way, k], bundle_r.at[way, k], gen, n)
 
     def early_copy(k, way):
-        ref = gath.at[slots[first[k]], y, 0]
+        ref = gath.at[slots[origin[k]], y, pl.ds(0, EARLY[k])]
         gen = z * NY + (y + SIDE[way]) % NY
         return remote(ref, ref, early_s.at[way, k], early_r.at[way, k], gen, n)
 
     def side_copy(m, way):
-        ref = gath.at[slots[m], y, pl.ds(1, 2)]
+        ref = gath.at[slots[m], y, late(source[m])]
         gen = z * NY + (y + SIDE[way]) % NY
         return remote(ref, ref, side_s.at[way, m], side_r.at[way, m], gen, n)
 
@@ -338,7 +343,7 @@
         return remote(ref, ref, relay_s.at[way, m], relay_r.at[way, m], gen, n)
 
     def send_sides(m):
-        for way in range(2 if m < RELAY else 3):
+        for way in range(2 if m in RELAY else 3):
             side_copy(m, way).start()
 
     def relay(m):
@@ -351,13 +356,13 @@
         tiles = [rmsg[k, m].astype(F32) for m in range(NNET)]
         for j in range(3):
             chunk = jnp.concatenate([t[:, SCN * j : SCN * (j + 1)] for t in tiles], axis=1)
-            gath[slots[first[k]], y, j] = chunk.astype(BF16)
+            gath[slots[origin[k]], y, j] = chunk.astype(BF16)
         for way in (2, 0, 1):
             early_copy(k, way).start()
         if k < 3:
             for way in (2, 3, 0, 1):
                 near_copy(k, way).start()
-        send_sides(first[k])
+        send_sides(origin[k])
 
     def bundle(k):
         for way in range(3):
@@ -388,8 +393,7 @@
     bundle(2)
     for way in range(4):
         arrive(1, way)
-        if way < 3:
-            relay((1, 2, 7)[way])
+    relay(7)
     for way in range(4):
         arrive(2, way)
     turn(7)
@@ -417,8 +421,8 @@
     groups = (range(0, 4), range(4, 8), range(8, 12), range(12, 16))
     for i, group in enumerate(groups):
         for m in group:
-            for way in range(2 if m < RELAY else 3):
-                (relay_copy if m < RELAY else side_copy)(m, way).wait_recv()
+            for way in range(2 if m in RELAY else 3):
+                (relay_copy if m in RELAY else side_copy)(m, way).wait_recv()
             for k in range(3):
                 if after[k] <= m < after[k] + 4:
                     bundle_copy(k, m - after[k]).wait_recv()
@@ -494,9 +498,9 @@
                 near_copy(k, way).wait_send()
                 bundle_copy(k, way).wait_send()
     for m in range(NZ):
-        for way in range(2 if m < RELAY else 3):
+        for way in range(2 if m in RELAY else 3):
             side_copy(m, way).wait_send()
-            if m < RELAY:
+            if m in RELAY:
                 relay_copy(m, way).wait_send()
     for q in tiles:
         core_copy(q).wait_send()
@@ -584,8 +588,8 @@
             dma((3, 4)),
             dma((3, NZ)),
             dma((3, NZ)),
-            dma((2, RELAY)),
-            dma((2, RELAY)),
+            dma((2, NZ)),
+            dma((2, NZ)),
             dma((2 * BUS // TILE,)),
             dma((2 * BUS // TILE,)),
             dma((2 * BUS // TILE,)),

time: 70.4 us -> 69.4 us (0.986)
  Pallas kernels: 68 us -> 67 us
    pallas_call x1, Pallas kernels: 68 us -> 67 us  [body(): pl.pallas_call(kernel, out_shape=jax.ShapeDtypeStruct(state.shape, F32),...]
where the time goes in v5:
time: 69.4 us; the launch traced here: 69.3 us
  Pallas kernels  67 us (97%)
  local copies, waits for them, and re-layouts  1.62 us (2%)
    pallas_call x1, Pallas kernels, body(): pl.pallas_call(kernel, out_shape=jax.ShapeDtypeStruct(state.shape, F32),...  67 us
    unnamed x1, local copies, waits for them, and re-layouts  1.62 us

profile of v5, /device:TPU:1, one launch (start us, length us, event | category | flops | bytes accessed | tf_op | source)
XLA Modules:
  0.0 69.3 jit_solution(8848514857307628720)
XLA Ops:
  0.7 67.0 %shard_map.91 = f32[6,32,256]{2,1,0:T(8,128)} custom-call(f32[6,32,256]{2,1,0:T(8,128)} %state_h.1, f32[13,256]{1,0:T(8,128)} %params_h.1, s32[1]{0:T(128)S(6)} %copy.11.count_h, s32[1,256]{1,0:T(1,128)} %bitcast.6, s32[1,256]{1,0:T(1,128)} %bitcast.7, bf16[2,8,192,384]{3,2,1,0:T(8,128)(2,1)} %bitcast.5, s32[1,32]{1,0:T(1,128)} %bitcast.8, s32[1,32]{1,0:T(1,128)} %bitcast.9, ...), custom_call_target="tpu_custom_call" | custom-call | tf_op jit(solution)/shard_map/pallas_call | solution.py:553
  67.6 1.6 %copy.12 = f32[6,32,256]{2,1,0:T(8,128)} copy(f32[6,32,256]{2,1,0:T(8,128)} %shard_map.91) | data formatting | bytes 393216

commit v6 on v5

--- a/solution.py
+++ b/solution.py
@@ -17,7 +17,7 @@
 SUB = BUS // NNET
 CAP = 6
 FAR = (0, 5, NZ - 5, NZ // 2)
-BACK = (0, 2, 1, 3)
+BACK = (0, 2, 1)
 NEAR = (1, NZ - 1, 2, NZ - 2)
 SIDE = (1, NY - 1, 2)
 EARLY = (1, 2, 1, 1)
@@ -122,6 +122,8 @@
     box_r,
     msg_s,
     msg_r,
+    far_s,
+    far_r,
     near_s,
     near_r,
     bundle_s,
@@ -287,7 +289,7 @@
     message = jnp.where(lane_iota((128, 128)) < 64, first, second).astype(BF16)
     smsg[...] = message.reshape(NNET, 16, 128)
 
-    for k in (0, 1, 2, 3):
+    for k in (0, 1, 2):
 
         def send_msg(i, carry, k=k):
             peer = (n + i) % NNET
@@ -327,6 +329,11 @@
         gen = ((z + NEAR[way]) % NZ) * NY + y
         return remote(ref, ref, bundle_s.at[way, k], bundle_r.at[way, k], gen, n)
 
+    def far_copy():
+        ref = gath.at[slots[0], y]
+        gen = ((z + FAR[3]) % NZ) * NY + y
+        return remote(ref, ref, far_s, far_r, gen, n)
+
     def early_copy(k, way):
         ref = gath.at[slots[origin[k]], y, pl.ds(0, EARLY[k])]
         gen = z * NY + (y + SIDE[way]) % NY
@@ -350,6 +357,14 @@
         for way in range(2):
             side_copy(m, way).wait_recv()
             relay_copy(m, way).start()
+
+    def spread(k):
+        for way in (2, 0, 1):
+            early_copy(k, way).start()
+        if k < 3:
+            for way in (2, 3, 0, 1):
+                near_copy(k, way).start()
+        send_sides(origin[k])
 
     def assemble(k):
         all_msgs(k).wait_recv()
@@ -357,12 +372,9 @@
         for j in range(3):
             chunk = jnp.concatenate([t[:, SCN * j : SCN * (j + 1)] for t in tiles], axis=1)
             gath[slots[origin[k]], y, j] = chunk.astype(BF16)
-        for way in (2, 0, 1):
-            early_copy(k, way).start()
-        if k < 3:
-            for way in (2, 3, 0, 1):
-                near_copy(k, way).start()
-        send_sides(origin[k])
+        spread(k)
+        if k == 0:
+            far_copy().start()
 
     def bundle(k):
         for way in range(3):
@@ -385,8 +397,9 @@
     relay(0)
     assemble(1)
     assemble(2)
-    assemble(3)
     turn(6)
+    far_copy().wait_recv()
+    spread(3)
     for m in (3, 4, 5, 6):
         relay(m)
     bundle(1)
@@ -407,11 +420,11 @@
     ).astype(BF16)
     bundle(3)
 
-    def product(group, rows=slice(None)):
+    def product(group):
         total = None
         for m in group:
             part = jnp.dot(
-                zt[slots[m], rows],
+                zt[slots[m]],
                 gath[slots[m]].reshape(BUS, NNET * SCN),
                 preferred_element_type=F32,
             )
@@ -428,7 +441,7 @@
                     bundle_copy(k, m - after[k]).wait_recv()
         if i == 0:
             acc[...] = product(group)
-        elif i < 3:
+        else:
             acc[...] += product(group)
 
     sib = n + 1 - 2 * c
@@ -449,7 +462,7 @@
 
     def finish(q):
         rows = slice(TILE * q, TILE * (q + 1))
-        whole = acc[rows] + product(groups[3], rows)
+        whole = acc[rows]
         vbuf[q] = whole.T.reshape(NX, NCORE, SCN, TILE)
         core_copy(q).start()
 
@@ -489,11 +502,12 @@
     rback[g, 0:3] = sback[g, 0:3]
 
     all_boxes.wait_send()
+    far_copy().wait_send()
     for k in range(4):
-        all_msgs(k).wait_send()
         for way in range(3):
             early_copy(k, way).wait_send()
         if k < 3:
+            all_msgs(k).wait_send()
             for way in range(4):
                 near_copy(k, way).wait_send()
                 bundle_copy(k, way).wait_send()
@@ -564,7 +578,7 @@
             pltpu.VMEM((NGEN, 4, 128), F32),
             pltpu.VMEM((NGEN, 4, 128), F32),
             pltpu.VMEM((NNET, 16, 128), BF16),
-            pltpu.VMEM((4, NNET, 16, 128), BF16),
+            pltpu.VMEM((3, NNET, 16, 128), BF16),
             pltpu.VMEM((2 * BUS // TILE, NX, NCORE, SCN, TILE), F32),
             pltpu.VMEM((2 * BUS // TILE, NX, SCN, TILE), F32),
             pltpu.VMEM((2 * BUS // TILE, NX, SCN, TILE), F32),
@@ -578,8 +592,10 @@
             dma((9,)),
             dma,
             dma,
-            dma((4,)),
-            dma((4,)),
+            dma((3,)),
+            dma((3,)),
+            dma,
+            dma,
             dma((4, 3)),
             dma((4, 3)),
             dma((4, 3)),

time: 69.4 us -> 69.1 us (level)
  no operation moved by 1% of the time
where the time goes in v6:
time: 69.1 us; the launch traced here: 68.7 us
  Pallas kernels  66.4 us (96%)
  local copies, waits for them, and re-layouts  1.62 us (2%)
    pallas_call x1, Pallas kernels, body(): pl.pallas_call(kernel, out_shape=jax.ShapeDtypeStruct(state.shape, F32),...  66.4 us
    unnamed x1, local copies, waits for them, and re-layouts  1.62 us

profile of v6, /device:TPU:1, one launch (start us, length us, event | category | flops | bytes accessed | tf_op | source)
XLA Modules:
  0.0 68.7 jit_solution(11218444068464367205)
XLA Ops:
  0.7 66.4 %shard_map.91 = f32[6,32,256]{2,1,0:T(8,128)} custom-call(f32[6,32,256]{2,1,0:T(8,128)} %state_h.1, f32[13,256]{1,0:T(8,128)} %params_h.1, s32[1]{0:T(128)S(6)} %copy.11.count_h, s32[1,256]{1,0:T(1,128)} %bitcast.6, s32[1,256]{1,0:T(1,128)} %bitcast.7, bf16[2,8,192,384]{3,2,1,0:T(8,128)(2,1)} %bitcast.5, s32[1,32]{1,0:T(1,128)} %bitcast.8, s32[1,32]{1,0:T(1,128)} %bitcast.9, ...), custom_call_target="tpu_custom_call" | custom-call | tf_op jit(solution)/shard_map/pallas_call | solution.py:567
  67.1 1.6 %copy.12 = f32[6,32,256]{2,1,0:T(8,128)} copy(f32[6,32,256]{2,1,0:T(8,128)} %shard_map.91) | data formatting | bytes 393216
